TPU v7x, 32 devices: a whole 2x2x4 slice. The times are simulated.
32 devices in a mesh: ctx: 8 (over z, y), fsdp: 4 (over x, core).
Axes of the slice: x: 2, y: 2, z: 4, core: 2. Of those that a mesh axis runs over, the one named last changes fastest.
Arguments:
- gate_in: bfloat16 [4096, 4096], P('ctx', 'fsdp'), may hold values from -6 to 6
- values: bfloat16 [4096, 4096], P('ctx', 'fsdp'), may hold values from -6 to 6
- gate_out: bfloat16 [4096, 4096], P('ctx', 'fsdp'), may hold values from -6 to 6
- bias: float32 [4096], P('fsdp'), may hold values from -4 to 4
- spectrum: bfloat16 [2, 8192, 4096], P(None, ('ctx', 'fsdp')), may hold values from -6 to 6
Outputs:
- gated: bfloat16 [4096, 4096], P('ctx', 'fsdp')
All inputs are finite; a program needn't handle non-finite values.
Results may differ from a plain program's by a relative error of at most 0.0049.
Values may be sent and summed in bfloat16 or wider, within the bound.
A program may use at most 128 MiB of HBM per device.

v0:
```python
import math

import jax
import jax.numpy as jnp
from jax import lax
from jax.sharding import PartitionSpec as P


def phase_angles(rows_side, cols_side, modulus):
    product = rows_side[:, None] * cols_side[None, :] % modulus
    return product.astype(jnp.float32) * (2.0 * math.pi / modulus)


def contract(matrix, operand):
    return jnp.einsum("kj,sjc->skc", matrix, operand, precision=lax.Precision.HIGHEST)


def mix_rows(matrix, operand):
    return jnp.einsum("kp,pjc->kjc", matrix, operand, precision=lax.Precision.HIGHEST)


def body(gate_in, values, gate_out, bias, spectrum):
    devices = lax.axis_size("ctx")
    rows_here = gate_in.shape[0]
    channels = gate_in.shape[1]
    block_rows = rows_here // devices
    length_total = 2 * rows_here * devices
    position = lax.axis_index("ctx")
    mixed = (gate_in.astype(jnp.float32) * values.astype(jnp.float32)).astype(jnp.bfloat16)
    mixed = lax.optimization_barrier(mixed)
    member = lax.axis_index("fsdp")
    filter_here = lax.dynamic_slice_in_dim(
        lax.all_gather(spectrum, "fsdp", axis=1, tiled=True), member * channels, channels, 2
    )
    source_index = jnp.arange(devices, dtype=jnp.int32)
    mirror_index = jnp.where(source_index == 0, devices, 2 * devices - source_index)
    radix_order = jnp.stack([source_index, mirror_index], axis=1).reshape(2 * devices)
    cross_angle = phase_angles(radix_order, source_index, 2 * devices)
    cross_cos = jnp.cos(cross_angle)
    cross_sin = jnp.sin(cross_angle)
    local_rows = position * block_rows + jnp.arange(block_rows, dtype=jnp.int32)
    twist_angle = (radix_order[:, None] * local_rows[None, :] % length_total).astype(
        jnp.float32
    ) * (2.0 * math.pi / length_total)
    twist_cos = jnp.cos(twist_angle)[:, :, None]
    twist_sin = jnp.sin(twist_angle)[:, :, None]
    source = mixed[None]
    width_now = source.shape[2]
    real_in = lax.all_to_all(
        source.reshape(source.shape[0], devices, block_rows, width_now),
        "ctx",
        split_axis=1,
        concat_axis=1,
        tiled=True,
    )[0].astype(jnp.float32)
    real_mix = mix_rows(cross_cos, real_in)
    imag_mix = -mix_rows(cross_sin, real_in)
    spread = jnp.stack(
        [real_mix * twist_cos + imag_mix * twist_sin, imag_mix * twist_cos - real_mix * twist_sin]
    )
    regrouped = lax.all_to_all(spread, "ctx", split_axis=1, concat_axis=2, tiled=True)
    row_index = jnp.arange(rows_here, dtype=jnp.int32)
    local_angle = phase_angles(row_index, row_index, rows_here)
    local_cos = jnp.cos(local_angle)
    local_sin = jnp.sin(local_angle)
    real_part = regrouped[0]
    imag_part = regrouped[1]
    freq_real = contract(local_cos, real_part) + contract(local_sin, imag_part)
    freq_imag = contract(local_cos, imag_part) - contract(local_sin, real_part)
    filter_float = filter_here.astype(jnp.float32).reshape(2, 2, rows_here, channels)
    prod_real = freq_real * filter_float[0] - freq_imag * filter_float[1]
    prod_imag = freq_real * filter_float[1] + freq_imag * filter_float[0]
    back_real = contract(local_cos, prod_real) - contract(local_sin, prod_imag)
    back_imag = contract(local_cos, prod_imag) + contract(local_sin, prod_real)
    pair_index = jnp.stack([position, jnp.where(position == 0, devices, 2 * devices - position)])
    back_angle = (pair_index[:, None] * row_index[None, :] % length_total).astype(jnp.float32) * (
        2.0 * math.pi / length_total
    )
    back_cos = jnp.cos(back_angle)[:, :, None]
    back_sin = jnp.sin(back_angle)[:, :, None]
    turned_real = back_real * back_cos - back_imag * back_sin
    turned_imag = back_real * back_sin + back_imag * back_cos
    stacked = jnp.stack([turned_real, turned_imag]).reshape(2, 2, devices, block_rows, width_now)
    inverse_angle = phase_angles(source_index, radix_order, 2 * devices)
    inverse_cos = jnp.cos(inverse_angle) / length_total
    inverse_sin = jnp.sin(inverse_angle) / length_total
    received = lax.all_to_all(stacked, "ctx", split_axis=2, concat_axis=1, tiled=True)
    real_block = received[0, :, 0]
    imag_block = received[1, :, 0]
    real_out = mix_rows(inverse_cos, real_block) - mix_rows(inverse_sin, imag_block)
    folded = real_out[None]
    restored = lax.all_to_all(folded, "ctx", split_axis=1, concat_axis=1, tiled=True)
    restored = restored.reshape(restored.shape[0], rows_here, width_now)
    convolved_part = restored[0]
    convolved = convolved_part + bias[None, :] * mixed.astype(jnp.float32)
    return (gate_out.astype(jnp.float32) * convolved).astype(jnp.bfloat16)


def solution(mesh):
    return jax.shard_map(
        body,
        mesh=mesh,
        in_specs=(
            P("ctx", "fsdp"),
            P("ctx", "fsdp"),
            P("ctx", "fsdp"),
            P("fsdp"),
            P(None, ("ctx", "fsdp"), None),
        ),
        out_specs=P("ctx", "fsdp"),
        check_vma=False,
    )
```

profile of v0, /device:TPU:0, one launch (start us, length us, event | category | flops | bytes accessed | tf_op | source)
XLA Modules:
  0.0 659.4 jit_solution(13994440347685935459)
XLA Ops:
  8.1 1.4 multiply_convert_fusion
  9.4 7.3 %all-to-all-start = ((bf16[1,8,64,1024]{3,2,0,1:T(8,128)(2,1)}), bf16[1,8,64,1024]{3,2,0,1:T(8,128)(2,1)S(1)}, u32[]{:S(2)}, u32[]{:S(2)}) async-start(bf16[1,8,64,1024]{3,2,0,1:T(8,128)(2,1)} %bitcast.3), calls=%async_computation | async-start | bytes 2097152 | tf_op jit(solution)/shard_map/all_to_all | solution.py:49
  17.2 25.3 %all-to-all-done = bf16[1,8,64,1024]{3,2,0,1:T(8,128)(2,1)S(1)} async-done(((bf16[1,8,64,1024]{3,2,0,1:T(8,128)(2,1)}), bf16[1,8,64,1024]{3,2,0,1:T(8,128)(2,1)S(1)}, u32[]{:S(2)}, u32[]{:S(2)}) %all-to-all-start) | async-done | bytes 1048608 | tf_op jit(solution)/shard_map/all_to_all | solution.py:49
  42.5 2.0 fusion.25
  44.5 2.9 add_bitcast_fusion
  47.5 1.7 pad_maximum_fusion
  49.1 8.1 %copy.55 = f32[2,16,64,1024]{3,2,0,1:T(8,128)} copy(f32[2,16,64,1024]{3,1,2,0:T(8,128)S(1)} %pad_maximum_fusion) | data formatting | bytes 16777216 | tf_op jit(solution)/shard_map/stack | solution.py:58
  57.2 5.1 all-to-all-start.1
  62.6 181.6 %all-to-all-done.1 = f32[2,16,64,1024]{3,2,0,1:T(8,128)} async-done(((f32[2,16,64,1024]{3,2,0,1:T(8,128)}), f32[2,16,64,1024]{3,2,0,1:T(8,128)}, u32[]{:S(2)}, u32[]{:S(2)}) %all-to-all-start.1) | async-done | bytes 8388640 | tf_op jit(solution)/shard_map/all_to_all | solution.py:61
  244.2 4.2 copy.56
  248.4 1.7 fusion.134
  251.2 1.4 copy-done
  252.6 17.0 %fusion.23 = f32[2,1024,512]{2,1,0:T(8,128)S(1)} fusion(f32[2,512,1024]{2,1,0:T(8,128)S(1)} %bitcast.102), kind=kOutput, calls=%fused_computation.42 | convolution fusion | flops 6446120960 | bytes 8388608 | tf_op jit(solution)/shard_map/kj,sjc->skc/dot_general | solution.py:15
  269.6 18.7 %fusion.21 = f32[2,1024,512]{2,1,0:T(8,128)} fusion(f32[2,512,1024]{2,1,0:T(8,128)S(1)} %bitcast.100), kind=kOutput, calls=%fused_computation.40 | convolution fusion | flops 6446120960 | bytes 8388608 | tf_op jit(solution)/shard_map/kj,sjc->skc/dot_general | solution.py:15
  288.3 18.5 %convolution_add_fusion.1 = f32[2,1024,512]{2,1,0:T(8,128)} fusion(f32[2,1024,512]{2,1,0:T(8,128)S(1)} %fusion.23, f32[2,512,1024]{2,1,0:T(8,128)S(1)} %bitcast.101), kind=kOutput, calls=%fused_computation.20 | convolution fusion | flops 6447169536 | bytes 12582912 | tf_op jit(solution)/shard_map/kj,sjc->skc/dot_general | solution.py:15
  306.9 3.2 dynamic-slice_convert_fusion
  310.1 4.1 fusion.133
  314.2 5.4 copy.64
  319.6 5.4 copy.61
  325.0 26.0 %fusion.4 = (f32[2,512,1024]{1,2,0:T(8,128)S(1)}, f32[2,512,1024]{1,2,0:T(8,128)S(1)}) fusion(f32[2,512,1024]{1,2,0:T(8,128)} %copy.64, f32[2,512,1024]{1,2,0:T(8,128)} %copy.61, f32[2,1024,512]{2,1,0:T(8,128)} %convolution_add_fusion.1, f32[2,1024,512]{2,1,0:T(8,128)} %fusion.21, f32[2,512,1024]{2,1,0:T(8,128)} %bitcast.103), kind=kOutput, calls=%fused_computation.8 | convolution fusion | flops 6453460992 | bytes 29360128 | tf_op jit(solution)/shard_map/kj,sjc->skc/dot_general | solution.py:15
  351.0 10.7 %fusion.19 = f32[2,1024,512]{1,2,0:T(8,128)S(1)} fusion(f32[2,512,1024]{1,2,0:T(8,128)S(1)} %get-tuple-element.5), kind=kOutput, calls=%fused_computation.38 | convolution fusion | flops 6446120960 | bytes 8388608 | tf_op jit(solution)/shard_map/kj,sjc->skc/dot_general | solution.py:15
  361.6 11.1 %fusion.17 = f32[2,1024,512]{1,2,0:T(8,128)S(1)} fusion(f32[2,512,1024]{1,2,0:T(8,128)S(1)} %get-tuple-element.6), kind=kOutput, calls=%fused_computation.36 | convolution fusion | flops 6446120960 | bytes 8388608 | tf_op jit(solution)/shard_map/kj,sjc->skc/dot_general | solution.py:15
  372.8 11.2 %convolution_subtract_fusion = f32[2,1024,512]{1,2,0:T(8,128)S(1)} fusion(f32[2,1024,512]{1,2,0:T(8,128)S(1)} %fusion.19, f32[2,512,1024]{1,2,0:T(8,128)S(1)} %get-tuple-element.6), kind=kOutput, calls=%fused_computation.18 | convolution fusion | flops 6447169536 | bytes 12582912 | tf_op jit(solution)/shard_map/kj,sjc->skc/dot_general | solution.py:15
  384.0 12.2 %multiply_subtract_fusion = (f32[2,1024,512]{1,2,0:T(8,128)S(1)}, f32[2,1024,512]{1,2,0:T(8,128)S(1)}) fusion(f32[2,1024,512]{1,2,0:T(8,128)S(1)} %convolution_subtract_fusion, f32[2,512]{1,0:T(2,128)S(1)} %get-tuple-element.20, f32[2,512]{1,0:T(2,128)S(1)} %get-tuple-element.19, f32[2,1024,512]{1,2,0:T(8,128)S(1)} %fusion.17, ...), kind=kOutput, calls=%fused_computation.13 | convolution fusion | flops 6453460992 | bytes 20979712 | tf_op jit(solution)/shard_map/kj,sjc->skc/dot_general | solution.py:15
  396.2 1.7 pad_maximum_fusion.1
  397.8 1.7 copy.84
  399.5 186.7 %all_to_all.40 = f32[2,2,8,64,1024]{4,3,1,0,2:T(8,128)S(1)} all-to-all(f32[2,2,8,64,1024]{4,3,1,0,2:T(8,128)S(1)} %copy.84), channel_id=1, replica_groups=mesh['ctx'=8,'fsdp'=4] {'ctx'}, dimensions={2} | all-to-all | bytes 16777216 | tf_op jit(solution)/shard_map/all_to_all | solution.py:87
  586.2 1.7 fusion.132
  587.9 4.4 fusion
  592.4 4.5 subtract_bitcast_fusion.1
  598.1 51.4 %all_to_all.41 = f32[1,8,64,1024]{3,2,0,1:T(8,128)S(1)} all-to-all(f32[1,8,64,1024]{3,2,0,1:T(8,128)S(1)} %copy.75), channel_id=1, replica_groups=mesh['ctx'=8,'fsdp'=4] {'ctx'}, dimensions={1} | all-to-all | bytes 4194304 | tf_op jit(solution)/shard_map/all_to_all | solution.py:92
  649.5 2.9 fusion.7
  (24 shorter events, 4.4 us)
Async XLA Ops:
  6.5 1.2 copy-start.1
  6.5 1.5 copy-start.2
  6.5 300.3 %all-gather.2.cloned.1.call-start = ((), (), s32[]{:S(2)}) async-start(), calls=%async_computation.4 | async-start | bytes 20971520 | tf_op jit(solution)/shard_map/all_gather | solution.py:33
  9.4 33.0 %all-to-all-start = ((bf16[1,8,64,1024]{3,2,0,1:T(8,128)(2,1)}), bf16[1,8,64,1024]{3,2,0,1:T(8,128)(2,1)S(1)}, u32[]{:S(2)}, u32[]{:S(2)}) async-start(bf16[1,8,64,1024]{3,2,0,1:T(8,128)(2,1)} %bitcast.3), calls=%async_computation | async-start | bytes 2097152 | tf_op jit(solution)/shard_map/all_to_all | solution.py:49
  57.2 186.9 %all-to-all-start.1 = ((f32[2,16,64,1024]{3,2,0,1:T(8,128)}), f32[2,16,64,1024]{3,2,0,1:T(8,128)}, u32[]{:S(2)}, u32[]{:S(2)}) async-start(f32[2,16,64,1024]{3,2,0,1:T(8,128)} %copy.55), calls=%async_computation.1 | async-start | bytes 16777216 | tf_op jit(solution)/shard_map/all_to_all | solution.py:61
  250.6 2.0 copy-start
  596.8 52.6 %copy-start.3 = (bf16[512,1024]{1,0:T(8,128)(2,1)S(1)}, bf16[512,1024]{1,0:T(8,128)(2,1)}, u32[]{:S(2)}) copy-start(bf16[512,1024]{1,0:T(8,128)(2,1)} %param.7) | copy-start | bytes 3145732
  596.9 52.6 %copy-start.4 = (f32[1024]{0:T(1024)S(1)}, f32[1024]{0:T(1024)}, u32[]{:S(2)}) copy-start(f32[1024]{0:T(1024)} %param.8) | copy-start | bytes 12292
Sparse Core Ops, SparseCore 0:
  8.9 108.6 all-gather.1
where the time goes:
time: 668 us; the launch traced here: 659 us
  blocking collectives  238 us (36%)
  waiting for transfers between devices  208 us (31%)
  matrix products  139 us (21%)
  local copies, waits for them, and re-layouts  36.9 us (6%)
  between operations  13.8 us (2%)
  starting transfers between devices  12.4 us (2%)
  other arithmetic  11.2 us (2%)
    all_to_all x1, blocking collectives, body(): lax.all_to_all(stacked, 'ctx', split_axis=2, concat_axis=1, tiled=True)  187 us
    all_to_all x1, waiting for transfers between devices, body(): lax.all_to_all(spread, 'ctx', split_axis=1, concat_axis=2, tiled=True)  182 us
    dot_general x8, matrix products, contract(): jnp.einsum('kj,sjc->skc', matrix, operand, precision=lax.Precision.HIGHEST)  125 us
    all_to_all x1, blocking collectives, body(): lax.all_to_all(folded, 'ctx', split_axis=1, concat_axis=1, tiled=True)  51.4 us
    all_to_all x1, waiting for transfers between devices, body(): lax.all_to_all(source.reshape(source.shape[0], devices, block_rows, width...  25.3 us
    dot_general x4, matrix products, mix_rows(): jnp.einsum('kp,pjc->kjc', matrix, operand, precision=lax.Precision.HIGHEST)  13.9 us
  transfers between devices with their start and end apart: 3, of which 2 were waited for; matrix products, arithmetic and copies ran while one was open for 12% of the time, Pallas kernels for 0%

commit v1 on v0

v1 whole, which is shorter than its diff:
```python
import functools
import math

import jax
import jax.numpy as jnp
import numpy as np
from jax import lax
from jax.experimental import pallas as pl
from jax.experimental.pallas import tpu as pltpu
from jax.sharding import Mesh, PartitionSpec as P


@functools.lru_cache(maxsize=None)
def transform_matrices(rows):
    j = np.arange(rows)
    angle = 2 * np.pi * (np.outer(j, j) % rows) / rows
    cos, sin = np.cos(angle), np.sin(angle)
    general = np.block([[cos, sin], [-sin, cos]])
    half = rows // 2
    m = np.arange(half)
    low = 2 * np.pi * (np.outer(m, j) % rows) / rows
    mid = 2 * np.pi * (np.outer(2 * m + 1, j) % (2 * rows)) / (2 * rows)
    zero = np.zeros((half, rows))
    low_sin = -np.sin(low)
    low_sin[0] = np.where(j % 2 == 0, 1.0, -1.0)
    first = np.block(
        [[np.cos(low), zero], [zero, np.cos(mid)], [low_sin, zero], [zero, -np.sin(mid)]]
    )
    both = np.stack([first, general])
    return both.astype(jnp.bfloat16), both.transpose(0, 2, 1).astype(jnp.bfloat16)


@functools.lru_cache(maxsize=None)
def mixing_weights(devices):
    c = np.arange(devices)
    angle = 2 * np.pi * (np.outer(c, c) % (2 * devices)) / (2 * devices)
    real, imag = np.cos(angle), -np.sin(angle)
    imag[0] = np.where(c % 2 == 0, 1.0, -1.0)
    return np.stack([real, imag]).astype(np.float32)


@functools.lru_cache(maxsize=None)
def twists(devices, rows):
    angle = 2 * np.pi * np.outer(np.arange(devices), np.arange(rows)) / (2 * devices * rows)
    return np.stack([np.cos(angle), np.sin(angle)], axis=1).astype(np.float32)


def convolve_kernel(scale, flag, weights, x, forward, inverse, twist, filt, out, total):
    c = pl.program_id(0)
    devices, rows, width = x.shape
    half = rows // 2

    mixed_real = jnp.zeros((rows, width), jnp.float32)
    mixed_imag = jnp.zeros((rows, width), jnp.float32)
    for n in range(devices):
        block = x[n].astype(jnp.float32)
        mixed_real += weights[0, c, n] * block
        mixed_imag += weights[1, c, n] * block
    tc = twist[0, 0]
    ts = twist[0, 1]
    turned = jnp.concatenate(
        [mixed_real * tc + mixed_imag * ts, mixed_imag * tc - mixed_real * ts]
    ).astype(jnp.bfloat16)
    freq = jnp.dot(forward[0], turned, preferred_element_type=jnp.float32)
    swap = flag[0]
    filt_real = jnp.concatenate([filt[0, swap, 0], filt[0, 1 - swap, 0]]).astype(jnp.float32)
    filt_imag = jnp.concatenate([filt[0, swap, 1], filt[0, 1 - swap, 1]]).astype(jnp.float32)
    fr, fi = freq[:rows], freq[rows:]
    single = jnp.logical_and(
        c == 0, lax.broadcasted_iota(jnp.int32, (rows, width), 0) == 0
    )
    cross = fi * filt_imag
    prod_real = fr * filt_real - jnp.where(single, 0.0, cross)
    prod_imag = jnp.where(single, cross, fr * filt_imag + fi * filt_real)
    prod = jnp.concatenate([prod_real, prod_imag]).astype(jnp.bfloat16)
    back = jnp.dot(inverse[0], prod, preferred_element_type=jnp.float32)
    br, bi = back[:rows], back[rows:]
    back_real = (br * tc - bi * ts) * scale
    back_imag = (br * ts + bi * tc) * scale

    @pl.when(c == 0)
    def _():
        for n in range(devices):
            total[n] = weights[0, c, n] * back_real + weights[1, c, n] * back_imag

    @pl.when(c > 0)
    def _():
        for n in range(devices):
            total[n] += weights[0, c, n] * back_real + weights[1, c, n] * back_imag

    @pl.when(c == devices - 1)
    def _():
        out[...] = total[...].astype(out.dtype)


def convolve(x, filt, flag):
    devices, rows, width = x.shape
    forward, inverse = transform_matrices(rows)
    weights = mixing_weights(devices)
    twist = np.broadcast_to(twists(devices, rows)[..., None], (devices, 2, rows, 1))
    twist = jnp.broadcast_to(jnp.asarray(twist), (devices, 2, rows, width))
    whole = lambda c: (0, 0, 0)
    matrix = pl.BlockSpec((1, 2 * rows, 2 * rows), lambda c: (jnp.minimum(c, 1), 0, 0))
    return pl.pallas_call(
        functools.partial(convolve_kernel, 1.0 / (2 * devices * rows)),
        grid=(devices,),
        in_specs=[
            pl.BlockSpec(memory_space=pltpu.SMEM),
            pl.BlockSpec(memory_space=pltpu.SMEM),
            pl.BlockSpec((devices, rows, width), whole),
            matrix,
            matrix,
            pl.BlockSpec((1, 2, rows, width), lambda c: (c, 0, 0, 0)),
            pl.BlockSpec((1, 2, 2, rows // 2, width), lambda c: (c, 0, 0, 0, 0)),
        ],
        out_specs=pl.BlockSpec((devices, rows, width), whole),
        out_shape=jax.ShapeDtypeStruct((devices, rows, width), jnp.bfloat16),
        scratch_shapes=[pltpu.VMEM((devices, rows, width), jnp.float32)],
        compiler_params=pltpu.CompilerParams(vmem_limit_bytes=56 * 2**20),
        cost_estimate=pl.CostEstimate(
            flops=16 * devices * rows * rows * width,
            bytes_accessed=16 * 2**20,
            transcendentals=0,
        ),
    )(flag, jnp.asarray(weights), x, jnp.asarray(forward), jnp.asarray(inverse), twist, filt)


def fold_filters(spectrum):
    hi, lo, position = lax.axis_index("hi"), lax.axis_index("lo"), lax.axis_index("ctx")
    devices = lax.axis_size("ctx")
    block = spectrum.shape[1]
    width = spectrum.shape[2] // 2
    first, second = spectrum[:, :, :width], spectrum[:, :, width:]
    upper = hi == 1
    kept = jnp.where(upper, second, first)
    sent = jnp.where(upper, first, second)
    got = lax.ppermute(sent, ("hi", "lo"), [(f, 3 - f) for f in range(4)])
    slot_a = jnp.where(upper, got, kept)
    slot_b = jnp.where(upper, kept, got)
    half = jnp.bitwise_xor(hi, lo)
    passed = jnp.where(half == 0, slot_b, slot_a)
    swapped = lax.ppermute(
        passed, ("ctx", "hi", "lo"), [(0, 1), (1, 0), (2, 3), (3, 2)]
    )
    edge = position == 0
    base = jnp.where(jnp.logical_and(edge, half == 1), slot_b, slot_a)
    mirrored = jnp.where(edge, swapped, slot_b)
    wrap = jnp.logical_and(edge, half == 0)
    row = lax.broadcasted_iota(jnp.int32, (block, block), 0)
    col = lax.broadcasted_iota(jnp.int32, (block, block), 1)
    flip = (row + col == jnp.where(wrap, block, block - 1)).astype(jnp.bfloat16)
    turned = jnp.einsum("ij,rjk->rik", flip, mirrored, preferred_element_type=jnp.float32)
    real = base[0].astype(jnp.float32) + turned[0]
    imag = base[1].astype(jnp.float32) - turned[1]
    at_edge = jnp.logical_and(wrap, lax.broadcasted_iota(jnp.int32, (block, 1), 0) == 0)
    imag = jnp.where(at_edge, mirrored[0, :1].astype(jnp.float32), imag)
    return jnp.stack([real, imag]).astype(jnp.bfloat16)


def body(gate_in, values, gate_out, bias, spectrum):
    devices = lax.axis_size("ctx")
    rows, channels = gate_in.shape
    width = channels // devices
    mixed = (gate_in.astype(jnp.float32) * values.astype(jnp.float32)).astype(jnp.bfloat16)
    mixed = lax.optimization_barrier(mixed)
    parts = mixed.reshape(rows, devices, width).transpose(1, 0, 2)
    sequence = lax.all_to_all(parts, "ctx", split_axis=0, concat_axis=0, tiled=True)

    folded = fold_filters(spectrum)
    block = folded.shape[1]
    pieces = folded.reshape(2, block, 2, devices, width).transpose(3, 2, 0, 1, 4)
    pieces = pieces.reshape(devices * 2, 2, block, width)
    filt = lax.all_to_all(pieces, ("ctx", "lo"), split_axis=0, concat_axis=0, tiled=True)
    filt = filt.reshape(devices, 2, 2, block, width)
    flag = lax.axis_index("hi").astype(jnp.int32).reshape(1)

    convolved = convolve(sequence, filt, flag)
    back = lax.all_to_all(convolved, "ctx", split_axis=0, concat_axis=0, tiled=True)
    back = back.transpose(1, 0, 2).reshape(rows, channels).astype(jnp.float32)
    total = back + bias[None, :] * mixed.astype(jnp.float32)
    return (gate_out.astype(jnp.float32) * total).astype(jnp.bfloat16)


def solution(mesh):
    ctx, fsdp = mesh.devices.shape
    split = Mesh(mesh.devices.reshape(ctx, fsdp // 2, 2), ("ctx", "hi", "lo"))
    tokens = P("ctx", ("hi", "lo"))
    return jax.shard_map(
        body,
        mesh=split,
        in_specs=(
            tokens,
            tokens,
            tokens,
            P(("hi", "lo")),
            P(None, ("ctx", "hi", "lo"), None),
        ),
        out_specs=tokens,
        check_vma=False,
    )
```

time: 668 us -> 233 us (0.35); the launches traced: 659 us -> 232 us
  blocking collectives: 238 us -> 51.1 us
  matrix products: 139 us -> 0.74 us
  waiting for transfers between devices: 208 us -> 88.5 us
  Pallas kernels: 0 us -> 27.8 us
  between operations: 13.8 us -> 0.1 us
  local copies, waits for them, and re-layouts: 36.9 us -> 29.1 us
    all_to_all x2 -> x1, blocking collectives: 238 us -> 51.1 us  [body(): lax.all_to_all(pieces, ('ctx', 'lo'), split_axis=0, concat_axis=0, tiled=...]
    all_to_all x2, waiting for transfers between devices: 207 us -> 42.1 us  [the longest x1 24.9 us: body(): lax.all_to_all(convolved, 'ctx', split_axis=0, concat_axis=0, tiled=True)]
    dot_general x12 -> x1, matrix products: 139 us -> 0.74 us  [fold_filters(): jnp.einsum('ij,rjk->rik', flip, mirrored, preferred_element_type=jnp.floa...]
    ppermute x0 -> x2, waiting for transfers between devices: none -> 46.3 us  [the longest x1 46.3 us: fold_filters(): got = lax.ppermute(sent, ('hi', 'lo'), [(f, 3 - f) for f in range(4)])]
    pallas_call x0 -> x1, Pallas kernels: none -> 27.8 us  [convolve(): pl.pallas_call(functools.partial(convolve_kernel, 1.0 / (2 * devices * ro...]
    unnamed x10 -> x17, local copies, waits for them, and re-layouts: 2.27 us -> 13.3 us
    squeeze x2 -> x0, local copies, waits for them, and re-layouts: 10.8 us -> none  [body(): prod_real = freq_real * filter_float[0] - freq_imag * filter_float[1]]
    another operation x3 -> x0, local copies, waits for them, and re-layouts: 9.84 us -> none  [the longest x1 8.1 us: body(): jnp.stack([real_mix * twist_cos + imag_mix * twist_sin, imag_mix * twist_...]
  transfers between devices with their start and end apart: 3 -> 4, of which waited for: 2 -> 3; matrix products, arithmetic and copies ran while one was open for 12% -> 7% of each run, Pallas kernels for 0% -> 0%
where the time goes in v1:
time: 233 us; the launch traced here: 232 us
  waiting for transfers between devices  88.5 us (38%)
  blocking collectives  51.1 us (22%)
  local copies, waits for them, and re-layouts  29.1 us (12%)
  Pallas kernels  27.8 us (12%)
  other arithmetic  17.5 us (8%)
  starting transfers between devices  16.9 us (7%)
    all_to_all x1, blocking collectives, body(): lax.all_to_all(pieces, ('ctx', 'lo'), split_axis=0, concat_axis=0, tiled=...  51.1 us
    ppermute x1, waiting for transfers between devices, fold_filters(): got = lax.ppermute(sent, ('hi', 'lo'), [(f, 3 - f) for f in range(4)])  46.3 us
    pallas_call x1, Pallas kernels, convolve(): pl.pallas_call(functools.partial(convolve_kernel, 1.0 / (2 * devices * ro...  27.8 us
    all_to_all x1, waiting for transfers between devices, body(): lax.all_to_all(convolved, 'ctx', split_axis=0, concat_axis=0, tiled=True)  24.9 us
    all_to_all x1, waiting for transfers between devices, body(): lax.all_to_all(parts, 'ctx', split_axis=0, concat_axis=0, tiled=True)  17.2 us
    unnamed x17, local copies, waits for them, and re-layouts  13.3 us
    all_to_all x1, starting transfers between devices, body(): lax.all_to_all(parts, 'ctx', split_axis=0, concat_axis=0, tiled=True)  5.8 us
    all_to_all x1, starting transfers between devices, body(): lax.all_to_all(convolved, 'ctx', split_axis=0, concat_axis=0, tiled=True)  5.13 us
  transfers between devices with their start and end apart: 4, of which 3 were waited for; matrix products, arithmetic and copies ran while one was open for 7% of the time, Pallas kernels for 0%

profile of v1, /device:TPU:0, one launch (start us, length us, event | category | flops | bytes accessed | tf_op | source)
XLA Modules:
  0.0 231.7 jit_solution(7786144026425559607)
XLA Ops:
  0.0 4.8 %fusion.8 = (bf16[2,256,2048]{2,1,0:T(8,128)(2,1)}, bf16[2,256,2048]{2,1,0:T(8,128)(2,1)}) fusion(bf16[2,256,4096]{2,1,0:T(8,128)(2,1)} %param.13), kind=kLoop, calls=%fused_computation.24 | loop fusion | bytes 8388608 | tf_op jit(solution)/shard_map/slice | solution.py:133
  4.8 2.8 %copy.22 = bf16[2,256,2048]{1,2,0:T(8,128)(2,1)S(1)} copy(bf16[2,256,2048]{2,1,0:T(8,128)(2,1)} %get-tuple-element.8) | data formatting | bytes 4194304
  7.6 4.6 %copy.23 = bf16[2,256,2048]{1,2,0:T(8,128)(2,1)} copy(bf16[2,256,2048]{2,1,0:T(8,128)(2,1)} %get-tuple-element.9) | data formatting | bytes 4194304
  12.2 1.6 broadcast_select_fusion.4
  13.8 4.0 %collective-permute-start = (bf16[2,256,2048]{1,2,0:T(8,128)(2,1)}, bf16[2,256,2048]{1,2,0:T(8,128)(2,1)}, u32[]{:S(2)}, u32[]{:S(2)}) collective-permute-start(bf16[2,256,2048]{1,2,0:T(8,128)(2,1)} %broadcast_select_fusion.4), channel_id=1, source_target_pairs={{0,3},{1,2},{2,1},{3,0},{4,7},{5,6},{6,5},{7,4},{8,11},{9,10},{10,... | collective-permute-start | bytes 6291464 | tf_op jit(solution)/shard_map/ppermute | solution.py:137
  17.8 46.3 %collective-permute-done = bf16[2,256,2048]{1,2,0:T(8,128)(2,1)} collective-permute-done((bf16[2,256,2048]{1,2,0:T(8,128)(2,1)}, bf16[2,256,2048]{1,2,0:T(8,128)(2,1)}, u32[]{:S(2)}, u32[]{:S(2)}) %collective-permute-start) | collective-permute-done | bytes 2097184 | tf_op jit(solution)/shard_map/ppermute | solution.py:137
  64.1 3.9 %broadcast_select_fusion.6 = (bf16[2,256,2048]{1,2,0:T(8,128)(2,1)}, bf16[2,256,2048]{1,2,0:T(8,128)(2,1)S(1)}, bf16[2,256,2048]{1,2,0:T(8,128)(2,1)S(1)}) fusion(pred[]{:T(512)S(6)} %and.20, bf16[2,256,2048]{1,2,0:T(8,128)(2,1)} %collective-permute-done, bf16[2,256,2048]{1,2,0:T(8,128)(2,1)} %copy-done, bf16[2,256,2048]{1,2,0:T(8,128)(2,1)} %copy.23, ...), kind=kLoop, calls=%fused_computation.18 | loop fusion | flops 4194304 | bytes 12582914 | tf_op jit(solution)/shard_map/jit(_where)/select_n | solution.py:146
  68.1 1.5 broadcast_select_fusion
  69.6 2.0 collective-permute-start.1
  71.6 1.3 copy.14
  72.9 2.3 copy.15
  75.2 1.8 multiply_convert_fusion
  77.0 1.3 copy.16
  78.4 5.8 %all-to-all-start = ((bf16[8,512,128]{2,1,0:T(8,128)(2,1)}), bf16[8,512,128]{2,1,0:T(8,128)(2,1)}, u32[]{:S(2)}, u32[]{:S(2)}) async-start(bf16[8,512,128]{2,1,0:T(8,128)(2,1)} %bitcast.26), calls=%async_computation | async-start | bytes 2097152 | tf_op jit(solution)/shard_map/all_to_all | solution.py:167
  84.2 1.8 broadcast_select_fusion.1
  86.2 0.7 convolution_bitcast_fusion
  87.0 0.8 copy-done.1
  87.8 0.3 fusion.2
  88.1 0.4 fusion.1
  88.5 1.5 maximum_bitcast_fusion
  90.0 3.0 %copy.19 = bf16[8,2,2,256,128]{4,3,2,1,0:T(8,128)(2,1)S(1)} copy(bf16[8,2,2,256,128]{3,4,0,1,2:T(8,128)(2,1)} %maximum_bitcast_fusion) | data formatting | bytes 4194304 | tf_op jit(solution)/shard_map/transpose | solution.py:171
  93.1 17.2 %all-to-all-done.x = bf16[8,512,128]{2,1,0:T(8,128)(2,1)} async-done(((bf16[8,512,128]{2,1,0:T(8,128)(2,1)}), bf16[8,512,128]{2,1,0:T(8,128)(2,1)}, u32[]{:S(2)}, u32[]{:S(2)}) %all-to-all-start) | async-done | bytes 1048608 | tf_op jit(solution)/shard_map/all_to_all | solution.py:167
  110.3 51.1 %all_to_all.15 = bf16[16,2,256,128]{3,2,1,0:T(8,128)(2,1)} all-to-all(bf16[16,2,256,128]{3,2,1,0:T(8,128)(2,1)S(1)} %bitcast.25), channel_id=1, replica_groups=mesh['ctx'=8,'hi'=2,'lo'=2] {'ctx','lo'}, dimensions={0} | all-to-all | bytes 4194304 | tf_op jit(solution)/shard_map/all_to_all | solution.py:173
  161.4 2.6 %broadcast_in_dim.25.twist = f32[8,2,512,128]{3,2,1,0:T(8,128)} broadcast(f32[8,2,512]{2,1,0:T(2,128)S(1)} %copy-done.4), dimensions={0,1,2} | broadcast | bytes 4227072 | tf_op jit(solution)/shard_map/broadcast_in_dim | solution.py:101
  163.9 27.8 %shard_map.91 = bf16[8,512,128]{2,1,0:T(8,128)(2,1)} custom-call(s32[1]{0:T(128)} %bitcast.flag, f32[2,8,8]{2,1,0:T(8,128)} %constant.30.clone.weights, bf16[8,512,128]{2,1,0:T(8,128)(2,1)} %all-to-all-done.x, bf16[2,1024,1024]{2,1,0:T(8,128)(2,1)} %constant.31.clone.forward, bf16[2,1024,1024]{2,1,0:T(8,128)(2,1)} %constant.32.clone.inverse, ...), custom_call_target="tpu_custom_call" | custom-call | flops 4294967296 | bytes 16777216 | tf_op jit(solution)/shard_map/pallas_call | solution.py:104
  191.8 5.1 %all-to-all-start.2 = ((bf16[8,512,128]{2,1,0:T(8,128)(2,1)}), bf16[8,512,128]{2,1,0:T(8,128)(2,1)S(1)}, u32[]{:S(2)}, u32[]{:S(2)}) async-start(bf16[8,512,128]{2,1,0:T(8,128)(2,1)} %shard_map.91), calls=%async_computation.2 | async-start | bytes 2097152 | tf_op jit(solution)/shard_map/all_to_all | solution.py:178
  196.9 1.3 copy.13
  198.2 24.9 %all-to-all-done.2 = bf16[8,512,128]{2,1,0:T(8,128)(2,1)S(1)} async-done(((bf16[8,512,128]{2,1,0:T(8,128)(2,1)}), bf16[8,512,128]{2,1,0:T(8,128)(2,1)S(1)}, u32[]{:S(2)}, u32[]{:S(2)}) %all-to-all-start.2) | async-done | bytes 1048608 | tf_op jit(solution)/shard_map/all_to_all | solution.py:178
  223.1 1.5 convert_bitcast_fusion
  224.6 1.9 copy.20
  226.5 2.9 %fusion.4 = bf16[512,1024]{0,1:T(8,128)(2,1)} fusion(f32[512,8,128]{0,2,1:T(8,128)S(1)} %copy.20, bf16[512,1024]{0,1:T(8,128)(2,1)S(1)} %multiply_convert_fusion, bf16[512,1024]{0,1:T(8,128)(2,1)} %copy.13, f32[1024]{0:T(1024)S(1)} %copy-done.5), kind=kLoop, calls=%fused_computation.9 | loop fusion | flops 3145728 | bytes 5246976 | tf_op jit(solution)/shard_map/convert_element_type | solution.py:181
  229.5 2.3 copy.21
  (14 shorter events, 0.3 us)
Async XLA Ops:
  7.6 4.6 %copy-start = (bf16[2,256,2048]{1,2,0:T(8,128)(2,1)}, bf16[2,256,2048]{1,2,0:T(8,128)(2,1)S(1)}, u32[]{:S(2)}) copy-start(bf16[2,256,2048]{1,2,0:T(8,128)(2,1)S(1)} %copy.22) | copy-start | bytes 6291460
  13.8 50.3 %collective-permute-start = (bf16[2,256,2048]{1,2,0:T(8,128)(2,1)}, bf16[2,256,2048]{1,2,0:T(8,128)(2,1)}, u32[]{:S(2)}, u32[]{:S(2)}) collective-permute-start(bf16[2,256,2048]{1,2,0:T(8,128)(2,1)} %broadcast_select_fusion.4), channel_id=1, source_target_pairs={{0,3},{1,2},{2,1},{3,0},{4,7},{5,6},{6,5},{7,4},{8,11},{9,10},{10,... | collective-permute-start | bytes 6291464 | tf_op jit(solution)/shard_map/ppermute | solution.py:137
  68.0 3.6 %copy-start.2 = (bf16[512,1024]{1,0:T(8,128)(2,1)S(1)}, bf16[512,1024]{1,0:T(8,128)(2,1)}, u32[]{:S(2)}) copy-start(bf16[512,1024]{1,0:T(8,128)(2,1)} %param.9) | copy-start | bytes 3145732
  69.6 14.6 %collective-permute-start.1 = (bf16[2,256,2048]{1,2,0:T(8,128)(2,1)}, bf16[2,256,2048]{1,2,0:T(8,128)(2,1)}, u32[]{:S(2)}, u32[]{:S(2)}) collective-permute-start(bf16[2,256,2048]{1,2,0:T(8,128)(2,1)} %broadcast_select_fusion), channel_id=1, source_target_pairs={{0,1},{1,0},{2,3},{3,2}} | collective-permute-start | bytes 6291464 | tf_op jit(solution)/shard_map/ppermute | solution.py:142
  78.4 31.9 %all-to-all-start = ((bf16[8,512,128]{2,1,0:T(8,128)(2,1)}), bf16[8,512,128]{2,1,0:T(8,128)(2,1)}, u32[]{:S(2)}, u32[]{:S(2)}) async-start(bf16[8,512,128]{2,1,0:T(8,128)(2,1)} %bitcast.26), calls=%async_computation | async-start | bytes 2097152 | tf_op jit(solution)/shard_map/all_to_all | solution.py:167
  86.2 1.6 copy-start.1
  110.3 51.1 %copy-start.4 = (f32[8,2,512]{2,1,0:T(2,128)S(1)}, f32[8,2,512]{2,1,0:T(2,128)}, u32[]{:S(2)}) copy-start(f32[8,2,512]{2,1,0:T(2,128)} %constant.33) | copy-start | bytes 98308
  191.8 5.1 %copy-start.3 = (bf16[512,1024]{1,0:T(8,128)(2,1)S(1)}, bf16[512,1024]{1,0:T(8,128)(2,1)}, u32[]{:S(2)}) copy-start(bf16[512,1024]{1,0:T(8,128)(2,1)} %param.11) | copy-start | bytes 3145732
  191.8 31.4 %all-to-all-start.2 = ((bf16[8,512,128]{2,1,0:T(8,128)(2,1)}), bf16[8,512,128]{2,1,0:T(8,128)(2,1)S(1)}, u32[]{:S(2)}, u32[]{:S(2)}) async-start(bf16[8,512,128]{2,1,0:T(8,128)(2,1)} %shard_map.91), calls=%async_computation.2 | async-start | bytes 2097152 | tf_op jit(solution)/shard_map/all_to_all | solution.py:178
  224.6 1.9 copy-start.5

commit v2 on v1

--- a/solution.py
+++ b/solution.py
@@ -97,8 +97,8 @@
     devices, rows, width = x.shape
     forward, inverse = transform_matrices(rows)
     weights = mixing_weights(devices)
-    twist = np.broadcast_to(twists(devices, rows)[..., None], (devices, 2, rows, 1))
-    twist = jnp.broadcast_to(jnp.asarray(twist), (devices, 2, rows, width))
+    twist = np.broadcast_to(twists(devices, rows)[..., None], (devices, 2, rows, width))
+    twist = jnp.asarray(np.ascontiguousarray(twist))
     whole = lambda c: (0, 0, 0)
     matrix = pl.BlockSpec((1, 2 * rows, 2 * rows), lambda c: (jnp.minimum(c, 1), 0, 0))
     return pl.pallas_call(
@@ -157,21 +157,241 @@
     return jnp.stack([real, imag]).astype(jnp.bfloat16)
 
 
+def exchange_kernel(gate_in, values, spectrum, sequence, filt, mixed, kept, got, swapped, pair,
+                    folded, kept_sem, far_send, far_recv, swap_send, swap_recv, fold_send,
+                    fold_recv, mix_send, mix_recv):
+    me, hi, lo = lax.axis_index("ctx"), lax.axis_index("hi"), lax.axis_index("lo")
+    devices, rows, width = sequence.shape
+    block = spectrum.shape[1]
+    group = devices * width
+    edge = me == 0
+    half = (hi + lo) % 2
+
+    def columns(side, c, l):
+        start = side * (2 * group) + l * group + c * width
+        return spectrum.at[:, :, pl.ds(pl.multiple_of(start, 128), width)]
+
+    def remote(src, dst, send, recv, target):
+        return pltpu.make_async_remote_copy(
+            src_ref=src, dst_ref=dst, send_sem=send, recv_sem=recv,
+            device_id=target, device_id_type=pl.DeviceIdType.MESH,
+        )
+
+    def keep(c, l):
+        return pltpu.make_async_copy(columns(hi, c, l), kept.at[c, l], kept_sem.at[c, l])
+
+    def far(c, l):
+        return remote(columns(1 - hi, c, l), got.at[c, l], far_send.at[c, l], far_recv.at[c, l],
+                      (me, 1 - hi, 1 - lo))
+
+    def swap(source, c, l):
+        return remote(source.at[c, l], swapped.at[c, l], swap_send.at[c, l], swap_recv.at[c, l],
+                      (me, hi, 1 - lo))
+
+    def fold(c, l):
+        return remote(folded.at[c, l], filt.at[me, lo], fold_send.at[c, l], fold_recv.at[me, lo],
+                      (c, hi, l))
+
+    def fold_here(c, l):
+        return pltpu.make_async_copy(folded.at[c, l], filt.at[me, lo], fold_send.at[c, l])
+
+    def mix(c):
+        return remote(mixed.at[c], sequence.at[me], mix_send.at[c], mix_recv.at[me], (c, hi, lo))
+
+    def mix_here():
+        return pltpu.make_async_copy(mixed.at[me], sequence.at[me], mix_send.at[me])
+
+    barrier = pltpu.get_barrier_semaphore()
+
+    @pl.loop(0, devices)
+    def _(c):
+        for l in range(2):
+            @pl.when(jnp.logical_or(c != me, lo != l))
+            def _():
+                pl.semaphore_signal(barrier, inc=1, device_id=(c, hi, l),
+                                    device_id_type=pl.DeviceIdType.MESH)
+
+    pl.semaphore_signal(barrier, inc=1, device_id=(me, 1 - hi, 1 - lo),
+                        device_id_type=pl.DeviceIdType.MESH)
+
+    @pl.loop(0, devices)
+    def _(t):
+        c = (me + 1 + t) % devices
+        for l in range(2):
+            keep(c, l).start()
+
+    pl.semaphore_wait(barrier, 2 * devices)
+
+    @pl.loop(0, devices)
+    def _(t):
+        c = (me + 1 + t) % devices
+        for l in range(2):
+            far(c, l).start()
+
+    @pl.loop(0, devices)
+    def _(t):
+        c = (me + 1 + t) % devices
+        place = pl.ds(pl.multiple_of(c * width, 128), width)
+        mixed[c] = (
+            gate_in[:, place].astype(jnp.float32) * values[:, place].astype(jnp.float32)
+        ).astype(jnp.bfloat16)
+
+        @pl.when(c != me)
+        def _():
+            mix(c).start()
+
+        @pl.when(c == me)
+        def _():
+            mix_here().start()
+
+    wrap = jnp.logical_and(edge, half == 0)
+    row = lax.broadcasted_iota(jnp.int32, (block, block), 0)
+    col = lax.broadcasted_iota(jnp.int32, (block, block), 1)
+    flip = jnp.where(row + col == jnp.where(wrap, block, block - 1), 1.0, 0.0).astype(jnp.bfloat16)
+    at_edge = jnp.logical_and(wrap, lax.broadcasted_iota(jnp.int32, (block, width), 0) == 0)
+    base_got = jnp.where(edge, lo, hi) == 1
+
+    @pl.loop(0, devices)
+    def _(t):
+        c = (me + 1 + t) % devices
+        for l in range(2):
+            keep(c, l).wait()
+
+            @pl.when(jnp.logical_and(edge, lo == 1))
+            def _():
+                swap(kept, c, l).start()
+
+        for l in range(2):
+            far(c, l).wait_recv()
+
+            @pl.when(jnp.logical_and(edge, lo == 0))
+            def _():
+                swap(got, c, l).start()
+
+        for l in range(2):
+            @pl.when(edge)
+            def _():
+                swap(kept, c, l).wait_recv()
+                pair[...] = swapped[c, l]
+
+            @pl.when(jnp.logical_and(me != 0, hi == 0))
+            def _():
+                pair[...] = got[c, l]
+
+            @pl.when(jnp.logical_and(me != 0, hi == 1))
+            def _():
+                pair[...] = kept[c, l]
+
+            base = jnp.where(base_got, got[c, l].astype(jnp.float32), kept[c, l].astype(jnp.float32))
+            turned_real = jnp.dot(flip, pair[0], preferred_element_type=jnp.float32)
+            turned_imag = jnp.dot(flip, pair[1], preferred_element_type=jnp.float32)
+            real = base[0] + turned_real
+            imag = jnp.where(at_edge, pair[0].astype(jnp.float32), base[1] - turned_imag)
+            folded[c, l, 0] = real.astype(jnp.bfloat16)
+            folded[c, l, 1] = imag.astype(jnp.bfloat16)
+            here = jnp.logical_and(c == me, lo == l)
+
+            @pl.when(here)
+            def _():
+                fold_here(c, l).start()
+
+            @pl.when(jnp.logical_not(here))
+            def _():
+                fold(c, l).start()
+
+    @pl.loop(0, devices)
+    def _(c):
+        @pl.when(c == me)
+        def _():
+            mix_here().wait()
+
+        @pl.when(c != me)
+        def _():
+            mix(c).wait_send()
+            remote(mixed.at[c], sequence.at[c], mix_send.at[c], mix_recv.at[c],
+                   (c, hi, lo)).wait_recv()
+
+        for l in range(2):
+            far(c, l).wait_send()
+
+            @pl.when(edge)
+            def _():
+                swap(kept, c, l).wait_send()
+
+            here = jnp.logical_and(c == me, lo == l)
+
+            @pl.when(here)
+            def _():
+                fold_here(c, l).wait()
+
+            @pl.when(jnp.logical_not(here))
+            def _():
+                fold(c, l).wait_send()
+                remote(folded.at[c, l], filt.at[c, l], fold_send.at[c, l], fold_recv.at[c, l],
+                       (c, hi, l)).wait_recv()
+
+
+def exchange(gate_in, values, spectrum):
+    devices = lax.axis_size("ctx")
+    rows, channels = gate_in.shape
+    width = channels // devices
+    block = spectrum.shape[1]
+    tile = (devices, 2, 2, block, width)
+    dma = pltpu.SemaphoreType.DMA
+    here = pl.BlockSpec(memory_space=pltpu.VMEM)
+    anywhere = pl.BlockSpec(memory_space=pl.ANY)
+    return pl.pallas_call(
+        exchange_kernel,
+        in_specs=[here, here, anywhere],
+        out_specs=[anywhere, anywhere],
+        out_shape=[
+            jax.ShapeDtypeStruct((devices, rows, width), jnp.bfloat16),
+            jax.ShapeDtypeStruct(tile, jnp.bfloat16),
+        ],
+        scratch_shapes=[
+            pltpu.VMEM((devices, rows, width), jnp.bfloat16),
+            pltpu.VMEM(tile, jnp.bfloat16),
+            pltpu.VMEM(tile, jnp.bfloat16),
+            pltpu.VMEM(tile, jnp.bfloat16),
+            pltpu.VMEM((2, block, width), jnp.bfloat16),
+            pltpu.VMEM(tile, jnp.bfloat16),
+            *[dma((devices, 2))] * 7,
+            dma((devices,)),
+            dma((devices,)),
+        ],
+        compiler_params=pltpu.CompilerParams(
+            collective_id=0, has_side_effects=True, vmem_limit_bytes=48 * 2**20
+        ),
+        cost_estimate=pl.CostEstimate(flops=10**9, bytes_accessed=16 * 2**20, transcendentals=0),
+    )(gate_in, values, spectrum)
+
+
+def exchange_small(mixed, spectrum):
+    devices = lax.axis_size("ctx")
+    rows, channels = mixed.shape
+    width = channels // devices
+    parts = mixed.reshape(rows, devices, width).transpose(1, 0, 2)
+    sequence = lax.all_to_all(parts, "ctx", split_axis=0, concat_axis=0, tiled=True)
+
+    folded = fold_filters(spectrum)
+    block = folded.shape[1]
+    pieces = folded.reshape(2, block, 2, devices, width).transpose(3, 2, 0, 1, 4)
+    pieces = pieces.reshape(devices * 2, 2, block, width)
+    filt = lax.all_to_all(pieces, ("ctx", "lo"), split_axis=0, concat_axis=0, tiled=True)
+    filt = filt.reshape(devices, 2, 2, block, width)
+    return sequence, filt
+
+
 def body(gate_in, values, gate_out, bias, spectrum):
     devices = lax.axis_size("ctx")
     rows, channels = gate_in.shape
     width = channels // devices
     mixed = (gate_in.astype(jnp.float32) * values.astype(jnp.float32)).astype(jnp.bfloat16)
     mixed = lax.optimization_barrier(mixed)
-    parts = mixed.reshape(rows, devices, width).transpose(1, 0, 2)
-    sequence = lax.all_to_all(parts, "ctx", split_axis=0, concat_axis=0, tiled=True)
-
-    folded = fold_filters(spectrum)
-    block = folded.shape[1]
-    pieces = folded.reshape(2, block, 2, devices, width).transpose(3, 2, 0, 1, 4)
-    pieces = pieces.reshape(devices * 2, 2, block, width)
-    filt = lax.all_to_all(pieces, ("ctx", "lo"), split_axis=0, concat_axis=0, tiled=True)
-    filt = filt.reshape(devices, 2, 2, block, width)
+    if width % 128 == 0:
+        sequence, filt = exchange(gate_in, values, spectrum)
+    else:
+        sequence, filt = exchange_small(mixed, spectrum)
     flag = lax.axis_index("hi").astype(jnp.int32).reshape(1)
 
     convolved = convolve(sequence, filt, flag)

time: 233 us -> 147 us (0.63)
  waiting for transfers between devices: 88.5 us -> 20.2 us
  Pallas kernels: 27.8 us -> 87.3 us
  blocking collectives: 51.1 us -> 0 us
  local copies, waits for them, and re-layouts: 29.1 us -> 13 us
  other arithmetic: 17.5 us -> 6.95 us
  starting transfers between devices: 16.9 us -> 19.3 us
    pallas_call x0 -> x1, Pallas kernels: none -> 59.5 us  [exchange(): pl.pallas_call(exchange_kernel, in_specs=[here, here, anywhere], out_spec...]
    all_to_all x1 -> x0, blocking collectives: 51.1 us -> none  [body(): lax.all_to_all(pieces, ('ctx', 'lo'), split_axis=0, concat_axis=0, tiled=...]
    ppermute x2 -> x0, waiting for transfers between devices: 46.3 us -> none  [the longest x1 46.3 us: fold_filters(): got = lax.ppermute(sent, ('hi', 'lo'), [(f, 3 - f) for f in range(4)])]
    all_to_all x1 -> x0, waiting for transfers between devices: 17.2 us -> none  [body(): lax.all_to_all(parts, 'ctx', split_axis=0, concat_axis=0, tiled=True)]
    all_to_all x1, starting transfers between devices: 5.13 us -> 19.3 us  [body(): lax.all_to_all(convolved, 'ctx', split_axis=0, concat_axis=0, tiled=True)]
    select_n x4 -> x0, other arithmetic: 8.88 us -> none  [the longest x1 3.95 us: fold_filters(): base = jnp.where(jnp.logical_and(edge, half == 1), slot_b, slot_a)]
    ppermute x2 -> x0, starting transfers between devices: 5.96 us -> none  [the longest x1 3.97 us: fold_filters(): got = lax.ppermute(sent, ('hi', 'lo'), [(f, 3 - f) for f in range(4)])]
    all_to_all x1 -> x0, starting transfers between devices: 5.8 us -> none  [body(): lax.all_to_all(parts, 'ctx', split_axis=0, concat_axis=0, tiled=True)]
  transfers between devices with their start and end apart: 4 -> 1, of which waited for: 3 -> 1; matrix products, arithmetic and copies ran while one was open for 7% -> 4% of each run, Pallas kernels for 0% -> 0%
where the time goes in v2:
time: 147 us
  Pallas kernels  87.3 us (59%)
  waiting for transfers between devices  20.2 us (14%)
  starting transfers between devices  19.3 us (13%)
  local copies, waits for them, and re-layouts  13 us (9%)
  other arithmetic  6.95 us (5%)
    pallas_call x1, Pallas kernels, exchange(): pl.pallas_call(exchange_kernel, in_specs=[here, here, anywhere], out_spec...  59.5 us
    pallas_call x1, Pallas kernels, convolve(): pl.pallas_call(functools.partial(convolve_kernel, 1.0 / (2 * devices * ro...  27.8 us
    all_to_all x1, waiting for transfers between devices, body(): lax.all_to_all(convolved, 'ctx', split_axis=0, concat_axis=0, tiled=True)  20.2 us
    all_to_all x1, starting transfers between devices, body(): lax.all_to_all(convolved, 'ctx', split_axis=0, concat_axis=0, tiled=True)  19.3 us
    unnamed x23, local copies, waits for them, and re-layouts  8.72 us
  transfers between devices with their start and end apart: 1, of which 1 were waited for; matrix products, arithmetic and copies ran while one was open for 4% of the time, Pallas kernels for 0%

profile of v2, /device:TPU:0, one launch (start us, length us, event | category | flops | bytes accessed | tf_op | source)
XLA Modules:
  0.0 146.8 jit_solution(12150107866758186483)
XLA Ops:
  0.0 0.0 copy-start
  0.0 1.2 copy-done
  1.2 0.0 copy-start.2
  1.2 1.2 copy-done.2
  2.5 59.5 %shard_map.91 = (bf16[8,512,128]{2,1,0:T(8,128)(2,1)S(1)}, bf16[8,2,2,256,128]{4,3,2,1,0:T(8,128)(2,1)S(1)}) custom-call(bf16[512,1024]{1,0:T(8,128)(2,1)S(1)} %copy-done, bf16[512,1024]{1,0:T(8,128)(2,1)S(1)} %copy-done.2, bf16[2,256,4096]{2,1,0:T(8,128)(2,1)} %spectrum.1), custom_call_target="tpu_custom_call" | custom-call | flops 1000000000 | bytes 16777216 | tf_op jit(solution)/shard_map/pallas_call | solution.py:343
  61.9 0.0 copy-start.4
  61.9 1.3 copy-done.4
  63.3 0.0 copy-start.5
  63.3 1.0 copy-done.5
  64.2 27.8 %shard_map.92 = bf16[8,512,128]{2,1,0:T(8,128)(2,1)} custom-call(s32[1]{0:T(128)} %bitcast.flag, f32[2,8,8]{2,1,0:T(8,128)} %constant.13.clone.weights, bf16[8,512,128]{2,1,0:T(8,128)(2,1)} %copy-done.5, bf16[2,1024,1024]{2,1,0:T(8,128)(2,1)} %constant.14.clone.forward, bf16[2,1024,1024]{2,1,0:T(8,128)(2,1)} %constant.15.clone.inverse, ...), custom_call_target="tpu_custom_call" | custom-call | flops 4294967296 | bytes 16777216 | tf_op jit(solution)/shard_map/pallas_call | solution.py:104
  92.0 0.0 copy-start.1
  92.1 0.0 copy-start.3
  92.1 19.3 %all-to-all-start = ((bf16[8,512,128]{2,1,0:T(8,128)(2,1)}), bf16[8,512,128]{2,1,0:T(8,128)(2,1)S(1)}, u32[]{:S(2)}, u32[]{:S(2)}) async-start(bf16[8,512,128]{2,1,0:T(8,128)(2,1)} %shard_map.92), calls=%async_computation | async-start | bytes 2097152 | tf_op jit(solution)/shard_map/all_to_all | solution.py:398
  111.4 0.0 copy-done.1
  111.4 1.3 copy.12
  112.7 0.0 copy-done.3
  112.7 0.0 copy-start.6
  112.7 1.3 copy.13
  114.0 0.0 copy-done.6
  114.0 0.0 copy-start.8
  114.0 2.6 %multiply_convert_fusion = bf16[512,1024]{0,1:T(8,128)(2,1)} fusion(bf16[512,1024]{0,1:T(8,128)(2,1)} %copy.13, bf16[512,1024]{0,1:T(8,128)(2,1)S(1)} %copy-done.6), kind=kLoop, calls=%fused_computation.4 | loop fusion | flops 2097152 | bytes 3145728 | tf_op jit(solution)/shard_map/convert_element_type | solution.py:389
  116.6 0.0 copy-done.8
  116.6 1.3 copy.10
  117.9 20.2 %all-to-all-done = bf16[8,512,128]{2,1,0:T(8,128)(2,1)S(1)} async-done(((bf16[8,512,128]{2,1,0:T(8,128)(2,1)}), bf16[8,512,128]{2,1,0:T(8,128)(2,1)S(1)}, u32[]{:S(2)}, u32[]{:S(2)}) %all-to-all-start) | async-done | bytes 1048608 | tf_op jit(solution)/shard_map/all_to_all | solution.py:398
  138.1 1.5 %convert_bitcast_fusion = f32[512,8,128]{2,0,1:T(8,128)} fusion(bf16[8,512,128]{2,1,0:T(8,128)(2,1)S(1)} %all-to-all-done), kind=kLoop, calls=%fused_computation.3 | loop fusion | flops 524288 | bytes 3145728 | tf_op jit(solution)/shard_map/convert_element_type | solution.py:399
  139.6 0.0 copy-start.7
  139.6 0.0 copy-start.9
  139.6 2.0 %copy.11 = f32[512,8,128]{0,2,1:T(8,128)S(1)} copy(f32[512,8,128]{2,0,1:T(8,128)} %convert_bitcast_fusion) | data formatting | bytes 4194304 | tf_op jit(solution)/shard_map/convert_element_type | solution.py:399
  141.6 0.0 copy-done.7
  141.6 0.0 copy-done.9
  141.6 2.9 %fusion.1 = bf16[512,1024]{0,1:T(8,128)(2,1)} fusion(f32[512,8,128]{0,2,1:T(8,128)S(1)} %copy.11, bf16[512,1024]{0,1:T(8,128)(2,1)S(1)} %copy-done.7, bf16[512,1024]{0,1:T(8,128)(2,1)} %copy.10, f32[1024]{0:T(1024)S(1)} %copy-done.9), kind=kLoop, calls=%fused_computation.2 | loop fusion | flops 3145728 | bytes 5246976 | tf_op jit(solution)/shard_map/convert_element_type | solution.py:401
  144.5 2.3 %copy.14 = bf16[512,1024]{1,0:T(8,128)(2,1)} copy(bf16[512,1024]{0,1:T(8,128)(2,1)} %fusion.1) | data formatting | bytes 2097152 | tf_op jit(solution)/shard_map/convert_element_type | solution.py:401
Async XLA Ops:
  0.0 1.2 copy-start
  1.2 1.2 copy-start.2
  61.9 1.3 copy-start.4
  63.3 1.0 copy-start.5
  92.0 19.3 %copy-start.1 = (bf16[512,1024]{1,0:T(8,128)(2,1)S(1)}, bf16[512,1024]{1,0:T(8,128)(2,1)}, u32[]{:S(2)}) copy-start(bf16[512,1024]{1,0:T(8,128)(2,1)} %gate_in.1) | copy-start | bytes 3145732
  92.1 20.7 %copy-start.3 = (bf16[512,1024]{1,0:T(8,128)(2,1)S(1)}, bf16[512,1024]{1,0:T(8,128)(2,1)}, u32[]{:S(2)}) copy-start(bf16[512,1024]{1,0:T(8,128)(2,1)} %values.1) | copy-start | bytes 3145732
  92.1 46.0 %all-to-all-start = ((bf16[8,512,128]{2,1,0:T(8,128)(2,1)}), bf16[8,512,128]{2,1,0:T(8,128)(2,1)S(1)}, u32[]{:S(2)}, u32[]{:S(2)}) async-start(bf16[8,512,128]{2,1,0:T(8,128)(2,1)} %shard_map.92), calls=%async_computation | async-start | bytes 2097152 | tf_op jit(solution)/shard_map/all_to_all | solution.py:398
  112.7 1.3 copy-start.6
  114.0 2.6 %copy-start.8 = (bf16[512,1024]{1,0:T(8,128)(2,1)S(1)}, bf16[512,1024]{1,0:T(8,128)(2,1)}, u32[]{:S(2)}) copy-start(bf16[512,1024]{1,0:T(8,128)(2,1)} %param.11) | copy-start | bytes 3145732
  139.6 2.0 %copy-start.7 = (bf16[512,1024]{0,1:T(8,128)(2,1)S(1)}, bf16[512,1024]{0,1:T(8,128)(2,1)}, u32[]{:S(2)}) copy-start(bf16[512,1024]{0,1:T(8,128)(2,1)} %multiply_convert_fusion) | copy-start | bytes 3145732
  139.6 2.0 %copy-start.9 = (f32[1024]{0:T(1024)S(1)}, f32[1024]{0:T(1024)}, u32[]{:S(2)}) copy-start(f32[1024]{0:T(1024)} %param.12) | copy-start | bytes 12292

commit v3 on v2

--- a/solution.py
+++ b/solution.py
@@ -157,9 +157,11 @@
     return jnp.stack([real, imag]).astype(jnp.bfloat16)
 
 
-def exchange_kernel(gate_in, values, spectrum, sequence, filt, mixed, kept, got, swapped, pair,
-                    folded, kept_sem, far_send, far_recv, swap_send, swap_recv, fold_send,
-                    fold_recv, mix_send, mix_recv):
+def fused_kernel(scale, weights, gate_in, values, gate_out, bias, spectrum, forward_in, inverse_in,
+                 twist_in, out, sequence, filt, mixed, kept, got, swapped, pair, folded, forward,
+                 inverse, twist, freq, total, leaving, arrived, kept_sem, far_send, far_recv,
+                 swap_send, swap_recv, fold_send, fold_recv, mix_send, mix_recv, back_send,
+                 back_recv, table_sem):
     me, hi, lo = lax.axis_index("ctx"), lax.axis_index("hi"), lax.axis_index("lo")
     devices, rows, width = sequence.shape
     block = spectrum.shape[1]
@@ -201,6 +203,17 @@
     def mix_here():
         return pltpu.make_async_copy(mixed.at[me], sequence.at[me], mix_send.at[me])
 
+    def give_back(n):
+        return remote(leaving.at[n], arrived.at[me], back_send.at[n], back_recv.at[me],
+                      (n, hi, lo))
+
+    tables = [
+        pltpu.make_async_copy(src, dst, table_sem.at[i])
+        for i, (src, dst) in enumerate(
+            ((forward_in, forward), (inverse_in, inverse), (twist_in, twist))
+        )
+    ]
+
     barrier = pltpu.get_barrier_semaphore()
 
     @pl.loop(0, devices)
@@ -244,6 +257,9 @@
         def _():
             mix_here().start()
 
+    for table in tables:
+        table.start()
+
     wrap = jnp.logical_and(edge, half == 0)
     row = lax.broadcasted_iota(jnp.int32, (block, block), 0)
     col = lax.broadcasted_iota(jnp.int32, (block, block), 1)
@@ -251,8 +267,7 @@
     at_edge = jnp.logical_and(wrap, lax.broadcasted_iota(jnp.int32, (block, width), 0) == 0)
     base_got = jnp.where(edge, lo, hi) == 1
 
-    @pl.loop(0, devices)
-    def _(t):
+    def fold_step(t):
         c = (me + 1 + t) % devices
         for l in range(2):
             keep(c, l).wait()
@@ -299,25 +314,72 @@
             def _():
                 fold(c, l).start()
 
+    def forward_step(c):
+        real = jnp.zeros((rows, width), jnp.float32)
+        imag = jnp.zeros((rows, width), jnp.float32)
+        for n in range(devices):
+            part = sequence[n].astype(jnp.float32)
+            real += weights[0, c, n] * part
+            imag += weights[1, c, n] * part
+        tc, ts = twist[c, 0], twist[c, 1]
+        turned = jnp.concatenate([real * tc + imag * ts, imag * tc - real * ts])
+        freq[c] = jnp.dot(
+            forward[jnp.minimum(c, 1)], turned.astype(jnp.bfloat16),
+            preferred_element_type=jnp.float32,
+        )
+
+    def inverse_step(c):
+        filt_real = jnp.concatenate([filt[c, hi, 0], filt[c, 1 - hi, 0]]).astype(jnp.float32)
+        filt_imag = jnp.concatenate([filt[c, hi, 1], filt[c, 1 - hi, 1]]).astype(jnp.float32)
+        fr, fi = freq[c, :rows], freq[c, rows:]
+        top = lax.broadcasted_iota(jnp.int32, (rows, width), 0) == 0
+        single = jnp.logical_and(c == 0, top)
+        cross = fi * filt_imag
+        prod_real = fr * filt_real - jnp.where(single, 0.0, cross)
+        prod_imag = jnp.where(single, cross, fr * filt_imag + fi * filt_real)
+        prod = jnp.concatenate([prod_real, prod_imag]).astype(jnp.bfloat16)
+        back = jnp.dot(inverse[jnp.minimum(c, 1)], prod, preferred_element_type=jnp.float32)
+        tc, ts = twist[c, 0] * scale, twist[c, 1] * scale
+        br, bi = back[:rows], back[rows:]
+        real = br * tc - bi * ts
+        imag = br * ts + bi * tc
+        for n in range(devices):
+            total[n] += weights[0, c, n] * real + weights[1, c, n] * imag
+
+    early = devices // 2
+
+    @pl.loop(0, early)
+    def _(t):
+        fold_step(t)
+
+    for table in tables:
+        table.wait()
+
     @pl.loop(0, devices)
     def _(c):
+        total[c] = jnp.zeros((rows, width), jnp.float32)
+
         @pl.when(c == me)
         def _():
             mix_here().wait()
 
         @pl.when(c != me)
         def _():
-            mix(c).wait_send()
             remote(mixed.at[c], sequence.at[c], mix_send.at[c], mix_recv.at[c],
                    (c, hi, lo)).wait_recv()
 
-        for l in range(2):
-            far(c, l).wait_send()
-
-            @pl.when(edge)
-            def _():
-                swap(kept, c, l).wait_send()
-
+    @pl.loop(early, devices)
+    def _(t):
+        fold_step(t)
+
+        @pl.loop(0, 2)
+        def _(i):
+            forward_step(2 * (t - early) + i)
+
+    @pl.loop(0, devices)
+    def _(s):
+        c = (me + (2 * devices - 1) - s) % devices
+        for l in range(2):
             here = jnp.logical_and(c == me, lo == l)
 
             @pl.when(here)
@@ -326,44 +388,108 @@
 
             @pl.when(jnp.logical_not(here))
             def _():
-                fold(c, l).wait_send()
                 remote(folded.at[c, l], filt.at[c, l], fold_send.at[c, l], fold_recv.at[c, l],
                        (c, hi, l)).wait_recv()
 
-
-def exchange(gate_in, values, spectrum):
+        inverse_step(c)
+
+    @pl.loop(0, devices)
+    def _(t):
+        n = (me + 1 + t) % devices
+        leaving[n] = total[n].astype(jnp.bfloat16)
+
+        @pl.when(n != me)
+        def _():
+            give_back(n).start()
+
+    @pl.loop(0, devices)
+    def _(s):
+        c = (me + (2 * devices) - s) % devices
+        place = pl.ds(pl.multiple_of(c * width, 128), width)
+
+        @pl.when(c == me)
+        def _():
+            arrived[c] = leaving[c]
+
+        @pl.when(c != me)
+        def _():
+            remote(leaving.at[c], arrived.at[c], back_send.at[c], back_recv.at[c],
+                   (c, hi, lo)).wait_recv()
+
+        skip = bias[:, place] * mixed[c].astype(jnp.float32)
+        out[:, place] = (
+            gate_out[:, place].astype(jnp.float32) * (arrived[c].astype(jnp.float32) + skip)
+        ).astype(out.dtype)
+
+    @pl.loop(0, devices)
+    def _(c):
+        @pl.when(c != me)
+        def _():
+            mix(c).wait_send()
+            give_back(c).wait_send()
+
+        for l in range(2):
+            far(c, l).wait_send()
+
+            @pl.when(edge)
+            def _():
+                swap(kept, c, l).wait_send()
+
+            @pl.when(jnp.logical_or(c != me, lo != l))
+            def _():
+                fold(c, l).wait_send()
+
+
+def fused(gate_in, values, gate_out, bias, spectrum):
     devices = lax.axis_size("ctx")
     rows, channels = gate_in.shape
     width = channels // devices
     block = spectrum.shape[1]
+    forward, inverse = transform_matrices(rows)
+    twist = np.broadcast_to(twists(devices, rows)[..., None], (devices, 2, rows, width))
     tile = (devices, 2, 2, block, width)
+    whole = (devices, rows, width)
     dma = pltpu.SemaphoreType.DMA
     here = pl.BlockSpec(memory_space=pltpu.VMEM)
     anywhere = pl.BlockSpec(memory_space=pl.ANY)
     return pl.pallas_call(
-        exchange_kernel,
-        in_specs=[here, here, anywhere],
-        out_specs=[anywhere, anywhere],
-        out_shape=[
-            jax.ShapeDtypeStruct((devices, rows, width), jnp.bfloat16),
-            jax.ShapeDtypeStruct(tile, jnp.bfloat16),
-        ],
+        functools.partial(fused_kernel, 1.0 / (2 * devices * rows)),
+        in_specs=[pl.BlockSpec(memory_space=pltpu.SMEM)] + [here] * 4 + [anywhere] * 4,
+        out_specs=here,
+        out_shape=jax.ShapeDtypeStruct((rows, channels), jnp.bfloat16),
         scratch_shapes=[
-            pltpu.VMEM((devices, rows, width), jnp.bfloat16),
+            pltpu.VMEM(whole, jnp.bfloat16),
+            pltpu.VMEM(tile, jnp.bfloat16),
+            pltpu.VMEM(whole, jnp.bfloat16),
             pltpu.VMEM(tile, jnp.bfloat16),
             pltpu.VMEM(tile, jnp.bfloat16),
             pltpu.VMEM(tile, jnp.bfloat16),
             pltpu.VMEM((2, block, width), jnp.bfloat16),
             pltpu.VMEM(tile, jnp.bfloat16),
+            pltpu.VMEM((2, 2 * rows, 2 * rows), jnp.bfloat16),
+            pltpu.VMEM((2, 2 * rows, 2 * rows), jnp.bfloat16),
+            pltpu.VMEM((devices, 2, rows, width), jnp.float32),
+            pltpu.VMEM((devices, 2 * rows, width), jnp.float32),
+            pltpu.VMEM(whole, jnp.float32),
+            pltpu.VMEM(whole, jnp.bfloat16),
+            pltpu.VMEM(whole, jnp.bfloat16),
             *[dma((devices, 2))] * 7,
-            dma((devices,)),
-            dma((devices,)),
+            *[dma((devices,))] * 4,
+            dma((3,)),
         ],
         compiler_params=pltpu.CompilerParams(
-            collective_id=0, has_side_effects=True, vmem_limit_bytes=48 * 2**20
+            collective_id=0, has_side_effects=True, vmem_limit_bytes=58 * 2**20
         ),
-        cost_estimate=pl.CostEstimate(flops=10**9, bytes_accessed=16 * 2**20, transcendentals=0),
-    )(gate_in, values, spectrum)
+        cost_estimate=pl.CostEstimate(
+            flops=16 * devices * rows * rows * width + 10**9,
+            bytes_accessed=24 * 2**20,
+            transcendentals=0,
+        ),
+    )(
+        jnp.asarray(mixing_weights(devices)), gate_in, values, gate_out, bias.reshape(1, channels),
+        spectrum, jnp.asarray(forward), jnp.asarray(inverse),
+        jnp.asarray(np.ascontiguousarray(twist)),
+    )
 
 
 def exchange_small(mixed, spectrum):
@@ -386,12 +512,11 @@
     devices = lax.axis_size("ctx")
     rows, channels = gate_in.shape
     width = channels // devices
+    if width % 128 == 0:
+        return fused(gate_in, values, gate_out, bias, spectrum)
     mixed = (gate_in.astype(jnp.float32) * values.astype(jnp.float32)).astype(jnp.bfloat16)
     mixed = lax.optimization_barrier(mixed)
-    if width % 128 == 0:
-        sequence, filt = exchange(gate_in, values, spectrum)
-    else:
-        sequence, filt = exchange_small(mixed, spectrum)
+    sequence, filt = exchange_small(mixed, spectrum)
     flag = lax.axis_index("hi").astype(jnp.int32).reshape(1)
 
     convolved = convolve(sequence, filt, flag)

time: 147 us -> 104 us (0.71)
  the two profiles are of different devices: /device:TPU:0 before, /device:TPU:29 now
where the time goes in v3:
time: 104 us
  Pallas kernels  102 us (98%)
  local copies, waits for them, and re-layouts  2.26 us (2%)
    pallas_call x1, Pallas kernels, fused(): pl.pallas_call(functools.partial(fused_kernel, 1.0 / (2 * devices * rows)...  102 us
    unnamed x1, local copies, waits for them, and re-layouts  2.26 us

profile of v3, /device:TPU:29, one launch (start us, length us, event | category | flops | bytes accessed | tf_op | source)
XLA Modules:
  0.0 103.9 jit_solution(811416640481920031)
XLA Ops:
  0.0 101.7 %shard_map.91 = bf16[512,1024]{1,0:T(8,128)(2,1)} custom-call(f32[2,8,8]{2,1,0:T(8,128)} %constant.8.clone.weights, bf16[512,1024]{1,0:T(8,128)(2,1)} %gate_in.1, bf16[512,1024]{1,0:T(8,128)(2,1)} %values.1, bf16[512,1024]{1,0:T(8,128)(2,1)} %gate_out.1, f32[1,1024]{1,0:T(1,128)} %bitcast.1, bf16[2,256,4096]{2,1,0:T(8,128)(2,1)} %spectrum.1, ...), custom_call_target="tpu_custom_call" | custom-call | flops 5294967296 | bytes 25165824 | tf_op jit(solution)/shard_map/pallas_call | solution.py:455
  101.7 2.3 %copy.11 = bf16[512,1024]{1,0:T(8,128)(2,1)} copy(bf16[512,1024]{1,0:T(8,128)(2,1)} %shard_map.91) | data formatting | bytes 2097152

commit v4 on v3

--- a/solution.py
+++ b/solution.py
@@ -169,6 +169,16 @@
     edge = me == 0
     half = (hi + lo) % 2
 
+    def offset(t):
+        step = (t + 1) // 2
+        return devices // 2 + (1 - 2 * (t % 2)) * step
+
+    def target(t):
+        return (me + offset(t)) % devices
+
+    def origin(t):
+        return (me + devices - offset(t)) % devices
+
     def columns(side, c, l):
         start = side * (2 * group) + l * group + c * width
         return spectrum.at[:, :, pl.ds(pl.multiple_of(start, 128), width)]
@@ -229,26 +239,23 @@
 
     @pl.loop(0, devices)
     def _(t):
-        c = (me + 1 + t) % devices
+        c = target(t)
         for l in range(2):
             keep(c, l).start()
 
-    pl.semaphore_wait(barrier, 2 * devices)
-
-    @pl.loop(0, devices)
-    def _(t):
-        c = (me + 1 + t) % devices
-        for l in range(2):
-            far(c, l).start()
-
-    @pl.loop(0, devices)
-    def _(t):
-        c = (me + 1 + t) % devices
+    @pl.loop(0, devices)
+    def _(c):
         place = pl.ds(pl.multiple_of(c * width, 128), width)
         mixed[c] = (
             gate_in[:, place].astype(jnp.float32) * values[:, place].astype(jnp.float32)
         ).astype(jnp.bfloat16)
 
+    pl.semaphore_wait(barrier, 2 * devices)
+
+    @pl.loop(0, devices)
+    def _(t):
+        c = target(t)
+
         @pl.when(c != me)
         def _():
             mix(c).start()
@@ -256,6 +263,9 @@
         @pl.when(c == me)
         def _():
             mix_here().start()
+
+        for l in range(2):
+            far(c, l).start()
 
     for table in tables:
         table.start()
@@ -268,7 +278,7 @@
     base_got = jnp.where(edge, lo, hi) == 1
 
     def fold_step(t):
-        c = (me + 1 + t) % devices
+        c = target(t)
         for l in range(2):
             keep(c, l).wait()
 
@@ -378,7 +388,7 @@
 
     @pl.loop(0, devices)
     def _(s):
-        c = (me + (2 * devices - 1) - s) % devices
+        c = origin(s)
         for l in range(2):
             here = jnp.logical_and(c == me, lo == l)
 
@@ -395,7 +405,7 @@
 
     @pl.loop(0, devices)
     def _(t):
-        n = (me + 1 + t) % devices
+        n = target(t)
         leaving[n] = total[n].astype(jnp.bfloat16)
 
         @pl.when(n != me)
@@ -404,7 +414,7 @@
 
     @pl.loop(0, devices)
     def _(s):
-        c = (me + (2 * devices) - s) % devices
+        c = origin(s)
         place = pl.ds(pl.multiple_of(c * width, 128), width)
 
         @pl.when(c == me)

time: 104 us -> 105 us (level)
  the two profiles are of different devices: /device:TPU:29 before, /device:TPU:19 now
where the time goes in v4:
time: 105 us
  Pallas kernels  102 us (97%)
  local copies, waits for them, and re-layouts  2.26 us (2%)
    pallas_call x1, Pallas kernels, fused(): pl.pallas_call(functools.partial(fused_kernel, 1.0 / (2 * devices * rows)...  102 us
    unnamed x1, local copies, waits for them, and re-layouts  2.26 us

profile of v4, /device:TPU:19, one launch (start us, length us, event | category | flops | bytes accessed | tf_op | source)
XLA Modules:
  0.0 104.7 jit_solution(13486641791859520010)
XLA Ops:
  0.0 102.4 %shard_map.91 = bf16[512,1024]{1,0:T(8,128)(2,1)} custom-call(f32[2,8,8]{2,1,0:T(8,128)} %constant.8.clone.weights, bf16[512,1024]{1,0:T(8,128)(2,1)} %gate_in.1, bf16[512,1024]{1,0:T(8,128)(2,1)} %values.1, bf16[512,1024]{1,0:T(8,128)(2,1)} %gate_out.1, f32[1,1024]{1,0:T(1,128)} %bitcast.1, bf16[2,256,4096]{2,1,0:T(8,128)(2,1)} %spectrum.1, ...), custom_call_target="tpu_custom_call" | custom-call | flops 5294967296 | bytes 25165824 | tf_op jit(solution)/shard_map/pallas_call | solution.py:465
  102.4 2.3 %copy.11 = bf16[512,1024]{1,0:T(8,128)(2,1)} copy(bf16[512,1024]{1,0:T(8,128)(2,1)} %shard_map.91) | data formatting | bytes 2097152
